TPU v7x, 256 devices: a whole 4x4x8 slice. The times are simulated.
256 devices in a mesh: rows: 32 (over x, y, core), cols: 8 (over z).
Axes of the slice: x: 4, y: 4, z: 8, core: 2. Of those that a mesh axis runs over, the one named last changes fastest.
Arguments:
- basis: float32 [512, 32768], P(None, ('cols', 'rows')), may hold values from -6 to 6
- tile_counts: int32 [8192, 128, 128], P(('rows', 'cols')), may hold values from 0 to 63
- tile_rows: int32 [8192], P(('rows', 'cols')), may hold values from 0 to 7
- tile_cols: int32 [8192], P(('rows', 'cols')), may hold values from 0 to 31
- tile_live: int32 [256], P(('rows', 'cols')), may hold values from 8 to 32, as said below
- marginals: int32 [32768], replicated, may hold values from 1 to 983040, as said below
Outputs:
- subspace: float32 [512, 32768], P(None, ('cols', 'rows'))
Inputs may be any that keep to these rules, and one draw needn't show every extreme that they name: `tile_live`: every list has at least a quarter of its 32 slots live; some list has all 32 live. `marginals`: A small multiplier times a power of four.
All inputs are finite; a program needn't handle non-finite values.
Results may differ from a plain program's by a relative error of at most 0.012.
The roundings to bfloat16 on the way count: a program that leaves them out, or rounds other values in their place, can miss the bound.
Values may be sent and summed in bfloat16 or wider, within the bound.
No kernel may reach another device: no remote copies, remote signals or barrier semaphores. Data moves between devices by JAX's collectives and lax.ppermute only.
A program may use at most 128 MiB of HBM per device.

v0:
```python
import math

import jax
import jax.numpy as jnp
from jax import lax
from jax.sharding import PartitionSpec as P

ITERS = 2


def block_terms(blocks, ppmi, tile_rows, tile_cols, row_blocks):
    picked = jnp.take(blocks, tile_cols, axis=1)
    products = jnp.einsum("ktc,trc->ktr", picked, ppmi, preferred_element_type=jnp.float32)
    onehot = (tile_rows[:, None] == jnp.arange(row_blocks, dtype=jnp.int32)[None, :]).astype(
        jnp.float32
    )
    return jnp.einsum(
        "ktr,ta->kar",
        products,
        onehot,
        precision=lax.Precision.HIGHEST,
        preferred_element_type=jnp.float32,
    )


def local(basis, tile_counts, tile_rows, tile_cols, tile_live, marginals):
    width_k = basis.shape[0]
    terms_here = basis.shape[1]
    tile_size = tile_counts.shape[1]
    capacity = tile_counts.shape[0]
    row_count = lax.axis_size("rows")
    col_count = lax.axis_size("cols")
    row_index = lax.axis_index("rows")
    col_index = lax.axis_index("cols")
    group_size = row_count * terms_here
    row_blocks = col_count * terms_here // tile_size
    marg_float = marginals.astype(jnp.float32)
    grand_total = jnp.sum(marg_float)
    log_margins = jnp.log(marg_float)
    row_logs = lax.dynamic_index_in_dim(
        log_margins.reshape(col_count, row_count, terms_here), row_index, 1, keepdims=False
    )
    col_logs = lax.dynamic_slice_in_dim(log_margins, col_index * group_size, group_size).reshape(
        -1, tile_size
    )
    live_tiles = tile_live[0]
    counts_float = tile_counts.astype(jnp.float32)
    log_ratio = (
        jnp.log(jnp.maximum(counts_float, 1.0))
        + jnp.log(grand_total)
        - jnp.take(row_logs, tile_rows, axis=0)[:, :, None]
        - jnp.take(col_logs, tile_cols, axis=0)[:, None, :]
    )
    position = jnp.arange(capacity, dtype=jnp.int32)
    keep_mask = (tile_counts > 0) & (position < live_tiles)[:, None, None]
    ppmi = jnp.where(keep_mask, jnp.maximum(log_ratio, 0.0), 0.0).astype(jnp.bfloat16)
    block_width = math.gcd(capacity, 32)
    current = basis
    for sweep_index in range(ITERS):
        gathered = lax.all_gather(current.astype(jnp.bfloat16), "rows", axis=1, tiled=True)
        blocks = gathered.reshape(width_k, -1, tile_size)

        def add_block(block_index, running):
            return running + block_terms(blocks, ppmi, tile_rows, tile_cols, row_blocks)

        zero_sum = jnp.zeros((width_k, row_blocks, tile_size), jnp.float32)
        partial_sum = lax.fori_loop(0, capacity // block_width, add_block, zero_sum)
        partial_sum = partial_sum.reshape(width_k, col_count * terms_here)
        own_share = lax.psum_scatter(partial_sum, "cols", scatter_dimension=1, tiled=True)
        local_gram = jnp.dot(
            own_share,
            own_share.T,
            precision=lax.Precision.HIGHEST,
            preferred_element_type=jnp.float32,
        )
        gram_matrix = lax.psum(local_gram, ("rows", "cols"))
        factor = jnp.linalg.cholesky(gram_matrix)
        current = jax.scipy.linalg.solve_triangular(factor, own_share, lower=True)
    return current


def solution(mesh):
    in_specs = (
        P(None, ("cols", "rows")),
        P(("rows", "cols"), None, None),
        P(("rows", "cols")),
        P(("rows", "cols")),
        P(("rows", "cols")),
        P(),
    )
    out_specs = P(None, ("cols", "rows"))
    return jax.shard_map(local, mesh=mesh, in_specs=in_specs, out_specs=out_specs, check_vma=False)
```

profile of v0, /device:TPU:1, one launch (start us, length us, event | category | flops | bytes accessed | tf_op | source)
XLA Modules:
  0.0 1093.9 jit_solution(6459230053988258891)
XLA Ops:
  6.5 1.7 copy.16
  8.3 1.6 convert_reduce_fusion
  14.6 50.7 %all-gather.3.cloned.1.call-done = bf16[512,4096]{0,1:T(8,128)(2,1)} async-done(((bf16[512,128]{0,1:T(8,128)(2,1)}), bf16[512,4096]{0,1:T(8,128)(2,1)}) %all-gather.3.cloned.1.call-update) | async-done | bytes 4194320 | tf_op jit(solution)/shard_map/all_gather | solution.py:60
  65.3 6.4 copy.17
  71.7 5.4 gather_fusion.2
  77.1 7.5 fusion.8
  84.6 10.3 copy.18
  94.8 5.1 fusion.83
  100.0 1.8 copy.34
  101.8 37.0 %reduce-scatter.3.cloned.1.call-done = f32[512,128]{1,0:T(8,128)} async-done(((f32[512,1024]{1,0:T(8,128)}), f32[512,128]{1,0:T(8,128)}) %reduce-scatter.3.cloned.1.call-update) | async-done | bytes 262160 | tf_op jit(solution)/shard_map/reduce_scatter | solution.py:69
  138.9 3.1 fusion.95
  142.8 259.1 %all-reduce.4.cloned.1.call-done = f32[512,512]{0,1:T(8,128)} async-done(((f32[512,512]{0,1:T(8,128)}), f32[512,512]{0,1:T(8,128)}) %all-reduce.4.cloned.1.call-update) | async-done | bytes 1048592 | tf_op jit(solution)/shard_map/psum | solution.py:76
  401.9 2.7 copy.20
  404.6 1.4 fusion.17
  406.0 1.0 copy-done.3
  407.0 11.7 %cholesky.286 = f32[128,128]{1,0:T(8,128)S(1)} custom-call(f32[128,128]{1,0:T(8,128)S(1)} %cholesky.426), custom_call_target="Cholesky" | custom-call | tf_op jit(solution)/shard_map/jit(cholesky)/cholesky | solution.py:77
  418.8 9.8 custom-call.27
  428.7 1.2 constant_dynamic-update-slice_fusion.5
  430.0 1.3 convolution_subtract_fusion.1
  431.2 11.7 %cholesky.305 = f32[128,128]{1,0:T(8,128)S(1)} custom-call(f32[128,128]{1,0:T(8,128)S(1)} %cholesky.430), custom_call_target="Cholesky" | custom-call | tf_op jit(solution)/shard_map/jit(cholesky)/cholesky | solution.py:77
  444.3 10.3 custom-call.28
  454.9 1.3 convolution_subtract_fusion.3
  456.8 13.2 %cholesky.326 = f32[128,128]{1,0:T(8,128)} custom-call(f32[128,128]{1,0:T(8,128)} %cholesky.435), custom_call_target="Cholesky" | custom-call | tf_op jit(solution)/shard_map/jit(cholesky)/cholesky | solution.py:77
  470.0 1.5 fusion.78
  472.2 11.3 %custom-call.29 = f32[1,128,128]{1,2,0:T(8,128)} custom-call(f32[1,128,128]{2,1,0:T(8,128)} %get-tuple-element.95), custom_call_target="InvertDiagBlocksLowerTriangular" | custom-call | tf_op jit(solution)/shard_map/jit(cholesky)/cholesky | solution.py:77
  483.4 1.0 convolution_dynamic-update-slice_fusion.3
  484.5 1.2 convolution_subtract_fusion.11
  485.7 11.7 %cholesky.343 = f32[128,128]{1,0:T(8,128)S(1)} custom-call(f32[128,128]{1,0:T(8,128)S(1)} %convolution_subtract_fusion.11), custom_call_target="Cholesky" | custom-call | tf_op jit(solution)/shard_map/jit(cholesky)/cholesky | solution.py:77
  500.8 1.1 select_select_fusion.1
  502.0 12.0 %while.4 = (s32[]{:T(128)}, f32[512,512]{1,0:T(8,128)}, s32[4,2]{0,1:T(2,128)S(1)}, f32[4,128,128]{2,1,0:T(8,128)S(1)}, s32[]{:T(128)}) while((s32[]{:T(128)}, f32[512,512]{1,0:T(8,128)}, s32[4,2]{0,1:T(2,128)S(1)}, f32[4,128,128]{2,1,0:T(8,128)S(1)}, s32[]{:T(128)}) %tuple.57), condition=%wide.while_cond, body=%wide.while_body.sunk | while | flops 2 | bytes 131181 | solution.py:78
  502.6 2.3 bitcast_dynamic-update-slice_fusion.4
  505.7 2.3 bitcast_dynamic-update-slice_fusion.4
  508.7 2.3 bitcast_dynamic-update-slice_fusion.4
  511.7 2.3 bitcast_dynamic-update-slice_fusion.4
  514.0 39.3 %custom-call.30 = f32[4,128,128]{1,2,0:T(8,128)S(1)} custom-call(f32[4,128,128]{2,1,0:T(8,128)S(1)} %get-tuple-element.58), custom_call_target="InvertDiagBlocksLowerTriangular" | custom-call | tf_op jit(solution)/shard_map/jit(_solve_triangular)/triangular_solve | solution.py:78
  553.6 1.0 convolution_subtract_fusion.7
  555.0 1.2 convolution_subtract_fusion.6
  556.4 1.2 convolution_subtract_fusion.10
  558.7 54.9 %all-gather.5.cloned.1.call-done = bf16[512,4096]{1,0:T(8,128)(2,1)} async-done(((bf16[512,128]{1,0:T(8,128)(2,1)}), bf16[512,4096]{1,0:T(8,128)(2,1)}) %all-gather.5.cloned.1.call-update) | async-done | bytes 4194320 | tf_op jit(solution)/shard_map/all_gather | solution.py:60
  613.7 5.3 copy_bitcast_fusion
  619.0 5.4 gather_fusion.3
  624.4 7.5 fusion.11
  631.8 10.3 copy.22
  642.1 5.1 fusion.81
  647.2 1.8 copy.33
  649.3 37.0 %reduce-scatter.5.cloned.1.call-done = f32[512,128]{1,0:T(8,128)} async-done(((f32[512,1024]{1,0:T(8,128)}), f32[512,128]{1,0:T(8,128)}) %reduce-scatter.5.cloned.1.call-update) | async-done | bytes 262160 | tf_op jit(solution)/shard_map/reduce_scatter | solution.py:69
  686.3 3.1 fusion.96
  689.4 260.6 %all-reduce.6.cloned.1.call-done = f32[512,512]{0,1:T(8,128)} async-done(((f32[512,512]{0,1:T(8,128)}), f32[512,512]{0,1:T(8,128)}) %all-reduce.6.cloned.1.call-update) | async-done | bytes 1048592 | tf_op jit(solution)/shard_map/psum | solution.py:76
  950.0 1.6 copy.24
  951.9 11.7 %cholesky.358 = f32[128,128]{1,0:T(8,128)S(1)} custom-call(f32[128,128]{1,0:T(8,128)S(1)} %cholesky.439), custom_call_target="Cholesky" | custom-call | tf_op jit(solution)/shard_map/jit(cholesky)/cholesky | solution.py:77
  963.8 9.8 custom-call.31
  974.3 11.7 %cholesky.377 = f32[128,128]{1,0:T(8,128)S(1)} custom-call(f32[128,128]{1,0:T(8,128)S(1)} %cholesky.443), custom_call_target="Cholesky" | custom-call | tf_op jit(solution)/shard_map/jit(cholesky)/cholesky | solution.py:77
  986.0 0.7 compare_reduce_fusion.2
  987.4 10.2 custom-call.32
  998.3 11.7 %cholesky.398 = f32[128,128]{1,0:T(8,128)S(1)} custom-call(f32[128,128]{1,0:T(8,128)S(1)} %cholesky.448), custom_call_target="Cholesky" | custom-call | tf_op jit(solution)/shard_map/jit(cholesky)/cholesky | solution.py:77
  1010.6 9.8 custom-call.33
  1021.0 11.9 %cholesky.415 = f32[128,128]{1,0:T(8,128)S(1)} custom-call(f32[128,128]{1,0:T(8,128)S(1)} %convolution_subtract_fusion.9), custom_call_target="Cholesky" | custom-call | tf_op jit(solution)/shard_map/jit(cholesky)/cholesky | solution.py:77
  1036.3 8.5 while.5
  1037.0 1.4 bitcast_dynamic-update-slice_fusion.5
  1039.1 1.4 bitcast_dynamic-update-slice_fusion.5
  1041.2 1.4 bitcast_dynamic-update-slice_fusion.5
  1043.4 1.4 bitcast_dynamic-update-slice_fusion.5
  1044.8 39.3 %custom-call.34 = f32[4,128,128]{1,2,0:T(8,128)S(1)} custom-call(f32[4,128,128]{2,1,0:T(8,128)S(1)} %get-tuple-element.59), custom_call_target="InvertDiagBlocksLowerTriangular" | custom-call | tf_op jit(solution)/shard_map/jit(_solve_triangular)/triangular_solve | solution.py:78
  1086.1 0.7 pad_maximum_fusion
  (118 shorter events, 22.1 us)
Async XLA Ops:
  6.5 58.7 %all-gather.3.cloned.1.call-start = ((), (), s32[]{:S(2)}) async-start(), calls=%async_computation.2 | async-start | bytes 4325376 | tf_op jit(solution)/shard_map/all_gather | solution.py:60
  8.3 130.6 %reduce-scatter.3.cloned.1.call-start = ((), (), s32[]{:S(2)}) async-start(), calls=%async_computation.3 | async-start | bytes 2359296 | tf_op jit(solution)/shard_map/reduce_scatter | solution.py:69
  11.9 59.8 %copy-start.10 = (s32[1024]{0:T(1024)}, s32[1024]{0:T(1024)S(1)}, u32[]{:S(2)}) copy-start(s32[1024]{0:T(1024)S(1)} %pad_clamp_fusion) | copy-start | bytes 12292
  13.7 63.3 %copy-start.13 = (pred[32]{0:T(512)(128)(4,1)}, pred[32]{0:T(512)(128)(4,1)S(1)}, u32[]{:S(2)}) copy-start(pred[32]{0:T(512)(128)(4,1)S(1)} %iota_compare_fusion.4) | copy-start | bytes 100
  14.4 62.7 %copy-start.8 = (pred[32]{0:T(512)(128)(4,1)}, pred[32]{0:T(512)(128)(4,1)S(1)}, u32[]{:S(2)}) copy-start(pred[32]{0:T(512)(128)(4,1)S(1)} %get-tuple-element.106) | copy-start | bytes 100
  14.6 62.5 %copy-start.6 = (f32[32,128]{1,0:T(8,128)}, f32[32,128]{1,0:T(8,128)S(1)}, u32[]{:S(2)}) copy-start(f32[32,128]{1,0:T(8,128)S(1)} %broadcast_select_fusion.1) | copy-start | bytes 49156
  71.7 5.4 copy-start
  84.6 10.3 copy-start.11
  101.8 300.1 %all-reduce.4.cloned.1.call-start = ((), (), s32[]{:S(2)}) async-start(), calls=%async_computation.4 | async-start | bytes 2097152 | tf_op jit(solution)/shard_map/psum | solution.py:76
  142.0 471.7 %all-gather.5.cloned.1.call-start = ((), (), s32[]{:S(2)}) async-start(), calls=%async_computation.5 | async-start | bytes 4325376 | tf_op jit(solution)/shard_map/all_gather | solution.py:60
  401.9 2.7 copy-start.1
  406.0 1.0 copy-start.3
  456.2 97.1 %copy-start.4 = (f32[512,128]{1,0:T(8,128)S(1)}, f32[512,128]{1,0:T(8,128)}, u32[]{:S(2)}) copy-start(f32[512,128]{1,0:T(8,128)} %reduce-scatter.3.cloned.1.call-done) | copy-start | bytes 786436
  497.4 4.5 copy-start.15
  558.7 127.6 %reduce-scatter.5.cloned.1.call-start = ((), (), s32[]{:S(2)}) async-start(), calls=%async_computation.6 | async-start | bytes 2359296 | tf_op jit(solution)/shard_map/reduce_scatter | solution.py:69
  619.0 5.4 copy-start.7
  619.0 5.4 copy-start.9
  619.0 5.4 copy-start.14
  631.8 10.3 copy-start.12
  649.1 300.9 %all-reduce.6.cloned.1.call-start = ((), (), s32[]{:S(2)}) async-start(), calls=%async_computation.7 | async-start | bytes 2097152 | tf_op jit(solution)/shard_map/psum | solution.py:76
  950.0 1.7 copy-start.2
  998.2 85.9 %copy-start.5 = (f32[512,128]{1,0:T(8,128)S(1)}, f32[512,128]{1,0:T(8,128)}, u32[]{:S(2)}) copy-start(f32[512,128]{1,0:T(8,128)} %reduce-scatter.5.cloned.1.call-done) | copy-start | bytes 786436
Sparse Core Ops, SparseCore 0:
  9.9 55.2 all-gather.2
  101.9 36.9 reduce-scatter.2
  144.3 257.5 all-reduce.3
  558.8 54.8 all-gather.4
  649.2 37.0 reduce-scatter.4
  692.5 257.4 all-reduce.5
where the time goes:
time: 1100 us; the launch traced here: 1090 us
  waiting for transfers between devices  699 us (64%)
  other arithmetic  251 us (23%)
  local copies, waits for them, and re-layouts  76.2 us (7%)
  matrix products  46 us (4%)
  between operations  20.7 us (2%)
    psum x2, waiting for transfers between devices, local(): gram_matrix = lax.psum(local_gram, ('rows', 'cols'))  520 us
    another operation x30, other arithmetic, local(): factor = jnp.linalg.cholesky(gram_matrix)  164 us
    all_gather x2, waiting for transfers between devices, local(): lax.all_gather(current.astype(jnp.bfloat16), 'rows', axis=1, tiled=True)  106 us
    another operation x6, other arithmetic, local(): current = jax.scipy.linalg.solve_triangular(factor, own_share, lower=True)  81.1 us
    reduce_scatter x2, waiting for transfers between devices, local(): lax.psum_scatter(partial_sum, 'cols', scatter_dimension=1, tiled=True)  74 us
  transfers between devices with their start and end apart: 6, of which 6 were waited for; matrix products, arithmetic and copies ran while one was open for 0% of the time, Pallas kernels for 0%

commit v1 on v0

v1 whole, which is shorter than its diff:
```python
import jax
import jax.numpy as jnp
from jax import lax
from jax.experimental import pallas as pl
from jax.experimental.pallas import tpu as pltpu
from jax.sharding import Mesh, PartitionSpec as P

ITERS = 2
HIGHEST = lax.Precision.HIGHEST
TILE = 128
SUB = 8
BLOCKS = 4
PAIRS = [(i, j) for i in range(BLOCKS) for j in range(i + 1)]
PLACE = {pair: n for n, pair in enumerate(PAIRS)}
HALF = len(PAIRS) // 2
VMEM_LIMIT = 56 * 1024 * 1024
ROWS = ("x", "y", "core")
PLANE = ("x", "y")
VMEM = pl.BlockSpec(memory_space=pltpu.VMEM)
SMEM = pl.BlockSpec(memory_space=pltpu.SMEM)


def dot_nt(a, b, precision=HIGHEST):
    return lax.dot_general(
        a, b, (((1,), (1,)), ((), ())), precision=precision, preferred_element_type=jnp.float32
    )


def dot_nn(a, b):
    return jnp.dot(a, b, precision=HIGHEST, preferred_element_type=jnp.float32)


def call(kernel, out_shape, in_specs, scratch=()):
    return pl.pallas_call(
        kernel,
        out_shape=out_shape,
        in_specs=in_specs,
        out_specs=VMEM,
        scratch_shapes=list(scratch),
        compiler_params=pltpu.CompilerParams(vmem_limit_bytes=VMEM_LIMIT),
    )


def multiply_kernel(live_ref, rows_ref, cols_ref, basis_ref, ppmi_ref, out_ref):
    out_ref[...] = jnp.zeros_like(out_ref)

    def add_tile(t, carry):
        r = rows_ref[t]
        product = dot_nt(basis_ref[cols_ref[t]], ppmi_ref[t], None)
        out_ref[r] = out_ref[r] + product
        return carry

    lax.fori_loop(0, live_ref[0], add_tile, 0)


def gram_kernel(core_ref, own_ref, other_ref, out_ref):
    for n in range(HALF):
        first, second = PAIRS[n], PAIRS[HALF + n]
        core = core_ref[0]
        i = pl.multiple_of(jnp.where(core == 0, first[0], second[0]) * TILE, TILE)
        j = pl.multiple_of(jnp.where(core == 0, first[1], second[1]) * TILE, TILE)
        out_ref[n] = dot_nt(own_ref[pl.ds(i, TILE), :], own_ref[pl.ds(j, TILE), :]) + dot_nt(
            other_ref[pl.ds(i, TILE), :], other_ref[pl.ds(j, TILE), :]
        )


def spread_row(x, m):
    return jnp.broadcast_to(x[m : m + 1, :], (SUB, TILE))


def spread_col(x, lane):
    return jnp.broadcast_to(x[:, lane : lane + 1], (SUB, TILE))


def factor_inverse(read, write):
    n = TILE // SUB
    a = [read(i) for i in range(n)]
    row = lax.broadcasted_iota(jnp.int32, (SUB, TILE), 0)
    lane = lax.broadcasted_iota(jnp.int32, (SUB, TILE), 1)
    m = [jnp.where(lane == row + SUB * i, 1.0, 0.0).astype(jnp.float32) for i in range(n)]
    for p in range(n):
        cols = [[spread_col(a[i], SUB * p + k) for i in range(p, n)] for k in range(SUB)]
        s = [[spread_row(cols[k][0], q) if q >= k else None for k in range(SUB)] for q in range(SUB)]
        u = [spread_row(a[p], k) for k in range(SUB)]
        v = [spread_row(m[p], k) for k in range(SUB)]
        following = [cols[k][1] for k in range(SUB)] if p + 1 < n else None
        low = [[None] * SUB for _ in range(SUB)]
        root = [None] * SUB
        for k in range(SUB):
            root[k] = lax.rsqrt(s[k][k])
            for q in range(k + 1, SUB):
                low[q][k] = s[q][k] * root[k]
            for q in range(k + 1, SUB):
                for t in range(k + 1, q + 1):
                    s[q][t] = s[q][t] - low[q][k] * low[t][k]
            u[k] = u[k] * root[k]
            v[k] = v[k] * root[k]
            for q in range(k + 1, SUB):
                u[q] = u[q] - low[q][k] * u[k]
                v[q] = v[q] - low[q][k] * v[k]
            if following is not None:
                following[k] = following[k] * root[k]
                for q in range(k + 1, SUB):
                    following[q] = following[q] - low[q][k] * following[k]
        for k in range(SUB):
            write(SUB * p + k, v[k])
        if p + 1 == n:
            break
        for k in range(SUB):
            a[p + 1] = a[p + 1] - following[k] * u[k]
        zu = [None] * SUB
        zv = [None] * SUB
        for k in reversed(range(SUB)):
            x, y = u[k], v[k]
            for q in range(k + 1, SUB):
                x = x - low[q][k] * zu[q]
                y = y - low[q][k] * zv[q]
            zu[k] = x * root[k]
            zv[k] = y * root[k]
        for i in range(p + 1, n):
            for k in range(SUB):
                if i > p + 1:
                    a[i] = a[i] - cols[k][i - p] * zu[k]
                m[i] = m[i] - cols[k][i - p] * zv[k]


def solve_kernel(core_ref, own_ref, other_ref, image_ref, out_ref, a_ref, w_ref):
    core = core_ref[0]
    for n in range(HALF):
        a_ref[core * HALF + n] = own_ref[n]
        a_ref[(1 - core) * HALF + n] = other_ref[n]
    factor = {}
    solved = []
    for j in range(BLOCKS):
        here = PLACE[j, j]

        def read(i):
            return a_ref[here, pl.ds(SUB * i, SUB), :]

        def write(r, value):
            w_ref[pl.ds(r, 1), :] = value[0:1, :]

        factor_inverse(read, write)
        inverse = w_ref[...]
        for i in range(j + 1, BLOCKS):
            factor[i, j] = dot_nt(a_ref[PLACE[i, j]], inverse)
        for i in range(j + 1, BLOCKS):
            for k in range(j + 1, i + 1):
                n = PLACE[i, k]
                a_ref[n] = a_ref[n] - dot_nt(factor[i, j], factor[k, j])
        rest = image_ref[pl.ds(TILE * j, TILE), :]
        for i in range(j):
            rest = rest - dot_nn(factor[j, i], solved[i])
        solved.append(dot_nn(inverse, rest))
        out_ref[pl.ds(TILE * j, TILE), :] = solved[j]


def swap_core(x):
    return lax.ppermute(x, "core", [(0, 1), (1, 0)])


def gram_sum(core, image):
    k, width = image.shape
    plane = lax.axis_size(PLANE)
    depth = lax.axis_size("z")
    part = call(
        gram_kernel, jax.ShapeDtypeStruct((HALF, TILE, TILE), jnp.float32), [SMEM, VMEM, VMEM]
    )(core, image, swap_core(image))
    part = part.reshape(plane, HALF * TILE // plane, TILE)
    part = jnp.sum(lax.all_to_all(part, PLANE, 0, 0), axis=0)
    part = jnp.broadcast_to(part[None], (depth,) + part.shape)
    part = jnp.sum(lax.all_to_all(part, "z", 0, 0), axis=0)
    part = jnp.broadcast_to(part[None], (plane,) + part.shape)
    part = lax.all_to_all(part, PLANE, 0, 0)
    part = part.reshape(HALF, TILE, TILE)
    return part, swap_core(part)


def local(basis, tile_counts, tile_rows, tile_cols, tile_live, marginals):
    width_k, terms_here = basis.shape
    capacity, tile_size, _ = tile_counts.shape
    row_count = lax.axis_size(ROWS)
    col_count = lax.axis_size("z")
    row_index = lax.axis_index(ROWS)
    col_index = lax.axis_index("z")
    core = lax.axis_index("core").astype(jnp.int32).reshape(1)
    group_size = row_count * terms_here
    gathered = lax.all_gather(basis.astype(jnp.bfloat16), ROWS, axis=0)
    marg_float = marginals.astype(jnp.float32)
    grand_total = jnp.sum(marg_float)
    log_margins = jnp.log(marg_float)
    row_logs = lax.dynamic_index_in_dim(
        log_margins.reshape(col_count, row_count, terms_here), row_index, 1, keepdims=False
    )
    col_logs = lax.dynamic_slice_in_dim(log_margins, col_index * group_size, group_size).reshape(
        -1, tile_size
    )
    log_ratio = (
        jnp.log(jnp.maximum(tile_counts.astype(jnp.float32), 1.0))
        + jnp.log(grand_total)
        - jnp.take(row_logs, tile_rows, axis=0)[:, :, None]
        - jnp.take(col_logs, tile_cols, axis=0)[:, None, :]
    )
    position = jnp.arange(capacity, dtype=jnp.int32)
    keep_mask = (tile_counts > 0) & (position < tile_live[0])[:, None, None]
    ppmi = jnp.where(keep_mask, jnp.maximum(log_ratio, 0.0), 0.0).astype(jnp.bfloat16)
    multiply = call(
        multiply_kernel,
        jax.ShapeDtypeStruct((col_count, width_k, terms_here), jnp.float32),
        [SMEM, SMEM, SMEM, VMEM, VMEM],
    )
    solve = call(
        solve_kernel,
        jax.ShapeDtypeStruct((width_k, terms_here), jnp.float32),
        [SMEM, VMEM, VMEM, VMEM],
        [pltpu.VMEM((len(PAIRS), TILE, TILE), jnp.float32), pltpu.VMEM((TILE, TILE), jnp.float32)],
    )
    for sweep_index in range(ITERS):
        if sweep_index:
            gathered = lax.all_gather(current.astype(jnp.bfloat16), ROWS, axis=0)
        partial_sum = multiply(tile_live, tile_rows, tile_cols, gathered, ppmi)
        image = lax.psum_scatter(partial_sum, "z", scatter_dimension=0)
        own, other = gram_sum(core, image)
        current = solve(core, own, other, image)
    return current


def solution(mesh):
    rows, cols = mesh.shape["rows"], mesh.shape["cols"]
    side = 4
    devices = mesh.devices.reshape(side, rows // (2 * side), 2, cols)
    inner = Mesh(devices, ("x", "y", "core", "z"))
    lists = (*ROWS, "z")
    terms = ("z", *ROWS)
    in_specs = (P(None, terms), P(lists, None, None), P(lists), P(lists), P(lists), P())
    return jax.shard_map(
        local, mesh=inner, in_specs=in_specs, out_specs=P(None, terms), check_vma=False
    )
```

time: 1100 us -> 371 us (0.34)
  waiting for transfers between devices: 699 us -> 175 us
  other arithmetic: 251 us -> 11.7 us
  blocking collectives: 0 us -> 76.6 us
  local copies, waits for them, and re-layouts: 76.2 us -> 4.07 us
  Pallas kernels: 0 us -> 65.6 us
  matrix products: 46 us -> 0 us
  starting transfers between devices: 0.72 us -> 19.2 us
    psum x2 -> x0, waiting for transfers between devices: 520 us -> none  [local(): gram_matrix = lax.psum(local_gram, ('rows', 'cols'))]
    another operation x36 -> x0, other arithmetic: 245 us -> none  [the longest x30 164 us: local(): factor = jnp.linalg.cholesky(gram_matrix)]
    all_to_all x0 -> x6, blocking collectives: none -> 76.6 us  [the longest x2 28.4 us: gram_sum(): part = jnp.sum(lax.all_to_all(part, PLANE, 0, 0), axis=0)]
    pallas_call x0 -> x6, Pallas kernels: none -> 65.6 us  [the longest x2 46.3 us: local(): current = solve(core, own, other, image)]
    dot_general x6 -> x0, matrix products: 31.3 us -> none  [the longest x2 15 us: block_terms(): jnp.einsum('ktc,trc->ktr', picked, ppmi, preferred_element_type=jnp.float32)]
    another operation x35 -> x0, local copies, waits for them, and re-layouts: 21.3 us -> none  [the longest x27 20.4 us: local(): current = jax.scipy.linalg.solve_triangular(factor, own_share, lower=True)]
    transpose x2 -> x0, local copies, waits for them, and re-layouts: 20.5 us -> none  [block_terms(): jnp.einsum('ktc,trc->ktr', picked, ppmi, preferred_element_type=jnp.float32)]
    ppermute x0 -> x4, starting transfers between devices: none -> 19 us  [swap_core(): return lax.ppermute(x, 'core', [(0, 1), (1, 0)])]
  transfers between devices with their start and end apart: 6 -> 8, of which waited for: 6 -> 8; matrix products, arithmetic and copies ran while one was open for 0% -> 3% of each run, Pallas kernels for 0% -> 0%
where the time goes in v1:
time: 371 us; the launch traced here: 367 us
  waiting for transfers between devices  175 us (47%)
  blocking collectives  76.6 us (21%)
  Pallas kernels  65.6 us (18%)
  starting transfers between devices  19.2 us (5%)
  between operations  14.7 us (4%)
  other arithmetic  11.7 us (3%)
  local copies, waits for them, and re-layouts  4.07 us (1%)
    reduce_scatter x2, waiting for transfers between devices, local(): image = lax.psum_scatter(partial_sum, 'z', scatter_dimension=0)  79 us
    pallas_call x2, Pallas kernels, local(): current = solve(core, own, other, image)  46.3 us
    all_gather x1, waiting for transfers between devices, local(): gathered = lax.all_gather(basis.astype(jnp.bfloat16), ROWS, axis=0)  46.2 us
    all_gather x1, waiting for transfers between devices, local(): gathered = lax.all_gather(current.astype(jnp.bfloat16), ROWS, axis=0)  44.3 us
    all_to_all x2, blocking collectives, gram_sum(): part = jnp.sum(lax.all_to_all(part, PLANE, 0, 0), axis=0)  28.4 us
    all_to_all x2, blocking collectives, gram_sum(): part = jnp.sum(lax.all_to_all(part, 'z', 0, 0), axis=0)  25.2 us
    all_to_all x2, blocking collectives, gram_sum(): part = lax.all_to_all(part, PLANE, 0, 0)  23 us
    ppermute x4, starting transfers between devices, swap_core(): return lax.ppermute(x, 'core', [(0, 1), (1, 0)])  19 us
  transfers between devices with their start and end apart: 8, of which 8 were waited for; matrix products, arithmetic and copies ran while one was open for 3% of the time, Pallas kernels for 0%

profile of v1, /device:TPU:1, one launch (start us, length us, event | category | flops | bytes accessed | tf_op | source)
XLA Modules:
  0.0 366.6 jit_solution(17647771634670747914)
XLA Ops:
  6.5 0.0 all-gather.5.cloned.1.call-start
  6.5 1.6 convert_element_type.15
  8.2 0.0 all-gather.5.cloned.1.call-update
  8.2 0.0 reduce-scatter.3.cloned.1.call-start
  8.9 1.5 convert_reduce_fusion
  11.0 0.7 compare_select_fusion.1
  11.7 0.6 gather_fusion
  12.3 0.7 compare_select_fusion
  13.0 0.6 gather_fusion.1
  13.5 0.7 compare_and_fusion.1
  14.2 0.7 compare_and_fusion
  14.9 0.1 broadcast_select_fusion
  14.9 4.1 %select_convert_fusion.ppmi_ref = bf16[32,128,128]{2,1,0:T(8,128)(2,1)} fusion(s32[32,128,128]{2,1,0:T(8,128)} %param.7, f32[32,128]{1,0:T(8,128)S(1)} %get-tuple-element.7, f32[32,128]{1,0:T(8,128)S(1)} %get-tuple-element.8, f32[]{:T(128)S(6)} %log.10, pred[32]{0:T(512)(128)(4,1)S(1)} %iota_compare_fusion), kind=kLoop, calls=%fused_computation.2 | loop fusion | flops 5242880 | bytes 3178532 | tf_op jit(solution)/shard_map/convert_element_type | solution.py:206
  19.0 46.2 %all-gather.5.cloned.1.call-done = bf16[16384,128]{1,0:T(8,128)(2,1)} async-done(((bf16[512,128]{1,0:T(8,128)(2,1)}), bf16[16384,128]{1,0:T(8,128)(2,1)}) %all-gather.5.cloned.1.call-update) | async-done | bytes 4194320 | tf_op jit(solution)/shard_map/all_gather | solution.py:188
  65.2 6.4 %shard_map.64 = f32[8,512,128]{2,1,0:T(8,128)} custom-call(s32[1]{0:T(128)} %copy.7.live_ref, s32[32]{0:T(128)} %rows_ref.3, s32[32]{0:T(128)} %cols_ref.3, bf16[32,512,128]{2,1,0:T(8,128)(2,1)} %bitcast.16, bf16[32,128,128]{2,1,0:T(8,128)(2,1)} %select_convert_fusion.ppmi_ref), custom_call_target="tpu_custom_call" | custom-call | tf_op jit(solution)/shard_map/pallas_call | solution.py:221
  71.7 0.0 reduce-scatter.3.cloned.1.call-update
  71.7 0.0 all-gather.7.cloned.1.call-start
  71.7 39.4 %reduce-scatter.3.cloned.1.call-done = f32[1,512,128]{2,1,0:T(8,128)} async-done(((f32[8,512,128]{2,1,0:T(8,128)}), f32[1,512,128]{2,1,0:T(8,128)}) %reduce-scatter.3.cloned.1.call-update) | async-done | bytes 262160 | tf_op jit(solution)/shard_map/reduce_scatter | solution.py:222
  111.2 4.7 %collective-permute-start = (f32[512,128]{1,0:T(8,128)}, f32[512,128]{1,0:T(8,128)S(1)}, u32[]{:S(2)}, u32[]{:S(2)}) collective-permute-start(f32[512,128]{1,0:T(8,128)} %bitcast.24), channel_id=1, source_target_pairs={{0,8},{8,0},{1,9},{9,1},{2,10},{10,2},{3,11},{11,3},{4,12},{12,4},... | collective-permute-start | bytes 786440 | tf_op jit(solution)/shard_map/ppermute | solution.py:159
  115.8 1.4 collective-permute-done.other_ref
  117.2 0.0 copy-start.4
  117.2 0.7 copy-done.4
  117.9 3.2 shard_map.65
  121.1 14.4 %all_to_all.30 = f32[16,40,128]{2,1,0:T(8,128)S(1)} all-to-all(f32[16,40,128]{2,1,0:T(8,128)} %bitcast.18), channel_id=1, replica_groups=mesh['x'=4,'y'=4,'core'=2,'z'=8] {'x','y'}, dimensions={0} | all-to-all | bytes 655360 | tf_op jit(solution)/shard_map/all_to_all | solution.py:170
  135.6 12.6 %all_to_all.31 = f32[8,40,128]{2,1,0:T(8,128)S(1)} all-to-all(f32[8,40,128]{2,1,0:T(8,128)S(1)} %broadcast_in_dim.56), channel_id=1, replica_groups=mesh['x'=4,'y'=4,'core'=2,'z'=8] {'z'}, dimensions={0} | all-to-all | bytes 327680 | tf_op jit(solution)/shard_map/all_to_all | solution.py:172
  148.3 11.5 %all_to_all.32 = f32[16,40,128]{2,1,0:T(8,128)S(1)} all-to-all(f32[16,40,128]{2,1,0:T(8,128)S(1)} %broadcast_in_dim.57), channel_id=1, replica_groups=mesh['x'=4,'y'=4,'core'=2,'z'=8] {'x','y'}, dimensions={0} | all-to-all | bytes 655360 | tf_op jit(solution)/shard_map/all_to_all | solution.py:174
  159.7 0.0 copy-start.1
  159.7 4.8 %collective-permute-start.1 = (f32[5,128,128]{2,1,0:T(8,128)S(1)}, f32[5,128,128]{2,1,0:T(8,128)S(1)}, u32[]{:S(2)}, u32[]{:S(2)}) collective-permute-start(f32[5,128,128]{2,1,0:T(8,128)S(1)} %bitcast.22), channel_id=1, source_target_pairs={{0,8},{8,0},{1,9},{9,1},{2,10},{10,2},{3,11},{11,3},{4,12},{12,4},... | collective-permute-start | bytes 983048 | tf_op jit(solution)/shard_map/ppermute | solution.py:159
  164.6 1.3 collective-permute-done.1.other_ref
  165.8 0.0 copy-done.1
  165.8 0.0 copy-start.3
  165.8 0.7 copy-done.3
  166.5 23.1 %shard_map.66 = f32[512,128]{1,0:T(8,128)} custom-call(s32[1]{0:T(128)} %bitcast.core_ref, f32[5,128,128]{2,1,0:T(8,128)} %bitcast.23, f32[5,128,128]{2,1,0:T(8,128)} %copy-done.3, f32[512,128]{1,0:T(8,128)} %bitcast.26), custom_call_target="tpu_custom_call" | custom-call | tf_op jit(solution)/shard_map/pallas_call | solution.py:224
  189.7 1.6 convert_element_type.19
  191.3 0.0 all-gather.7.cloned.1.call-update
  191.3 0.0 reduce-scatter.5.cloned.1.call-start
  191.3 44.3 %all-gather.7.cloned.1.call-done = bf16[16384,128]{1,0:T(8,128)(2,1)} async-done(((bf16[512,128]{1,0:T(8,128)(2,1)}), bf16[16384,128]{1,0:T(8,128)(2,1)}) %all-gather.7.cloned.1.call-update) | async-done | bytes 4194320 | tf_op jit(solution)/shard_map/all_gather | solution.py:220
  235.6 6.4 %shard_map.67 = f32[8,512,128]{2,1,0:T(8,128)} custom-call(s32[1]{0:T(128)} %copy.7.live_ref, s32[32]{0:T(128)} %rows_ref.3, s32[32]{0:T(128)} %cols_ref.3, bf16[32,512,128]{2,1,0:T(8,128)(2,1)} %bitcast.17, bf16[32,128,128]{2,1,0:T(8,128)(2,1)} %select_convert_fusion.ppmi_ref), custom_call_target="tpu_custom_call" | custom-call | tf_op jit(solution)/shard_map/pallas_call | solution.py:221
  242.1 0.0 reduce-scatter.5.cloned.1.call-update
  242.1 39.6 %reduce-scatter.5.cloned.1.call-done = f32[1,512,128]{2,1,0:T(8,128)} async-done(((f32[8,512,128]{2,1,0:T(8,128)}), f32[1,512,128]{2,1,0:T(8,128)}) %reduce-scatter.5.cloned.1.call-update) | async-done | bytes 262160 | tf_op jit(solution)/shard_map/reduce_scatter | solution.py:222
  281.6 5.0 %collective-permute-start.2 = (f32[512,128]{1,0:T(8,128)}, f32[512,128]{1,0:T(8,128)S(1)}, u32[]{:S(2)}, u32[]{:S(2)}) collective-permute-start(f32[512,128]{1,0:T(8,128)} %bitcast.27), channel_id=1, source_target_pairs={{0,8},{8,0},{1,9},{9,1},{2,10},{10,2},{3,11},{11,3},{4,12},{12,4},... | collective-permute-start | bytes 786440 | tf_op jit(solution)/shard_map/ppermute | solution.py:159
  286.6 1.4 collective-permute-done.2.other_ref
  288.0 0.0 copy-start.5
  288.0 0.7 copy-done.5
  288.7 3.2 shard_map.68
  291.9 14.0 %all_to_all.33 = f32[16,40,128]{2,1,0:T(8,128)S(1)} all-to-all(f32[16,40,128]{2,1,0:T(8,128)} %bitcast.19), channel_id=1, replica_groups=mesh['x'=4,'y'=4,'core'=2,'z'=8] {'x','y'}, dimensions={0} | all-to-all | bytes 655360 | tf_op jit(solution)/shard_map/all_to_all | solution.py:170
  306.0 12.6 %all_to_all.34 = f32[8,40,128]{2,1,0:T(8,128)S(1)} all-to-all(f32[8,40,128]{2,1,0:T(8,128)S(1)} %broadcast_in_dim.58), channel_id=1, replica_groups=mesh['x'=4,'y'=4,'core'=2,'z'=8] {'z'}, dimensions={0} | all-to-all | bytes 327680 | tf_op jit(solution)/shard_map/all_to_all | solution.py:172
  318.6 11.5 %all_to_all.35 = f32[16,40,128]{2,1,0:T(8,128)S(1)} all-to-all(f32[16,40,128]{2,1,0:T(8,128)S(1)} %broadcast_in_dim.59), channel_id=1, replica_groups=mesh['x'=4,'y'=4,'core'=2,'z'=8] {'x','y'}, dimensions={0} | all-to-all | bytes 655360 | tf_op jit(solution)/shard_map/all_to_all | solution.py:174
  330.1 0.0 copy-start
  330.1 4.5 %collective-permute-start.3 = (f32[5,128,128]{2,1,0:T(8,128)S(1)}, f32[5,128,128]{2,1,0:T(8,128)S(1)}, u32[]{:S(2)}, u32[]{:S(2)}) collective-permute-start(f32[5,128,128]{2,1,0:T(8,128)S(1)} %bitcast.20), channel_id=1, source_target_pairs={{0,8},{8,0},{1,9},{9,1},{2,10},{10,2},{3,11},{11,3},{4,12},{12,4},... | collective-permute-start | bytes 983048 | tf_op jit(solution)/shard_map/ppermute | solution.py:159
  334.6 1.3 collective-permute-done.3.other_ref
  335.9 0.0 copy-done
  335.9 0.0 copy-start.2
  335.9 0.7 copy-done.2
  336.6 23.2 %shard_map.69 = f32[512,128]{1,0:T(8,128)} custom-call(s32[1]{0:T(128)} %bitcast.core_ref, f32[5,128,128]{2,1,0:T(8,128)} %bitcast.21, f32[5,128,128]{2,1,0:T(8,128)} %copy-done.2, f32[512,128]{1,0:T(8,128)} %bitcast.29), custom_call_target="tpu_custom_call" | custom-call | tf_op jit(solution)/shard_map/pallas_call | solution.py:224
  (13 shorter events, 0.2 us)
Async XLA Ops:
  6.5 58.7 %all-gather.5.cloned.1.call-start = ((), (), s32[]{:S(2)}) async-start(), calls=%async_computation.10 | async-start | bytes 4325376 | tf_op jit(solution)/shard_map/all_gather | solution.py:188
  8.2 103.0 %reduce-scatter.3.cloned.1.call-start = ((), (), s32[]{:S(2)}) async-start(), calls=%async_computation.8 | async-start | bytes 2359296 | tf_op jit(solution)/shard_map/reduce_scatter | solution.py:222
  71.7 163.9 %all-gather.7.cloned.1.call-start = ((), (), s32[]{:S(2)}) async-start(), calls=%async_computation.11 | async-start | bytes 4325376 | tf_op jit(solution)/shard_map/all_gather | solution.py:220
  111.2 6.1 %collective-permute-start = (f32[512,128]{1,0:T(8,128)}, f32[512,128]{1,0:T(8,128)S(1)}, u32[]{:S(2)}, u32[]{:S(2)}) collective-permute-start(f32[512,128]{1,0:T(8,128)} %bitcast.24), channel_id=1, source_target_pairs={{0,8},{8,0},{1,9},{9,1},{2,10},{10,2},{3,11},{11,3},{4,12},{12,4},... | collective-permute-start | bytes 786440 | tf_op jit(solution)/shard_map/ppermute | solution.py:159
  117.2 0.7 copy-start.4
  159.7 6.1 %copy-start.1 = (f32[16,40,128]{2,1,0:T(8,128)}, f32[16,40,128]{2,1,0:T(8,128)S(1)}, u32[]{:S(2)}) copy-start(f32[16,40,128]{2,1,0:T(8,128)S(1)} %all_to_all.32) | copy-start | bytes 983044
  159.7 6.1 %collective-permute-start.1 = (f32[5,128,128]{2,1,0:T(8,128)S(1)}, f32[5,128,128]{2,1,0:T(8,128)S(1)}, u32[]{:S(2)}, u32[]{:S(2)}) collective-permute-start(f32[5,128,128]{2,1,0:T(8,128)S(1)} %bitcast.22), channel_id=1, source_target_pairs={{0,8},{8,0},{1,9},{9,1},{2,10},{10,2},{3,11},{11,3},{4,12},{12,4},... | collective-permute-start | bytes 983048 | tf_op jit(solution)/shard_map/ppermute | solution.py:159
  165.8 0.7 copy-start.3
  191.3 90.4 %reduce-scatter.5.cloned.1.call-start = ((), (), s32[]{:S(2)}) async-start(), calls=%async_computation.9 | async-start | bytes 2359296 | tf_op jit(solution)/shard_map/reduce_scatter | solution.py:222
  281.6 6.4 %collective-permute-start.2 = (f32[512,128]{1,0:T(8,128)}, f32[512,128]{1,0:T(8,128)S(1)}, u32[]{:S(2)}, u32[]{:S(2)}) collective-permute-start(f32[512,128]{1,0:T(8,128)} %bitcast.27), channel_id=1, source_target_pairs={{0,8},{8,0},{1,9},{9,1},{2,10},{10,2},{3,11},{11,3},{4,12},{12,4},... | collective-permute-start | bytes 786440 | tf_op jit(solution)/shard_map/ppermute | solution.py:159
  288.0 0.7 copy-start.5
  330.1 5.8 %copy-start = (f32[16,40,128]{2,1,0:T(8,128)}, f32[16,40,128]{2,1,0:T(8,128)S(1)}, u32[]{:S(2)}) copy-start(f32[16,40,128]{2,1,0:T(8,128)S(1)} %all_to_all.35) | copy-start | bytes 983044
  330.1 5.8 %collective-permute-start.3 = (f32[5,128,128]{2,1,0:T(8,128)S(1)}, f32[5,128,128]{2,1,0:T(8,128)S(1)}, u32[]{:S(2)}, u32[]{:S(2)}) collective-permute-start(f32[5,128,128]{2,1,0:T(8,128)S(1)} %bitcast.20), channel_id=1, source_target_pairs={{0,8},{8,0},{1,9},{9,1},{2,10},{10,2},{3,11},{11,3},{4,12},{12,4},... | collective-permute-start | bytes 983048 | tf_op jit(solution)/shard_map/ppermute | solution.py:159
  335.9 0.7 copy-start.2
Sparse Core Ops, SparseCore 0:
  9.9 55.2 all-gather.4
  71.8 39.2 reduce-scatter.2
  191.4 44.1 all-gather.6
  242.2 39.4 reduce-scatter.4

commit v2 on v1

--- a/solution.py
+++ b/solution.py
@@ -13,7 +13,6 @@
 PAIRS = [(i, j) for i in range(BLOCKS) for j in range(i + 1)]
 PLACE = {pair: n for n, pair in enumerate(PAIRS)}
 HALF = len(PAIRS) // 2
-VMEM_LIMIT = 56 * 1024 * 1024
 ROWS = ("x", "y", "core")
 PLANE = ("x", "y")
 VMEM = pl.BlockSpec(memory_space=pltpu.VMEM)
@@ -30,14 +29,14 @@
     return jnp.dot(a, b, precision=HIGHEST, preferred_element_type=jnp.float32)
 
 
-def call(kernel, out_shape, in_specs, scratch=()):
+def call(kernel, out_shape, in_specs, scratch=(), mib=16):
     return pl.pallas_call(
         kernel,
         out_shape=out_shape,
         in_specs=in_specs,
         out_specs=VMEM,
         scratch_shapes=list(scratch),
-        compiler_params=pltpu.CompilerParams(vmem_limit_bytes=VMEM_LIMIT),
+        compiler_params=pltpu.CompilerParams(vmem_limit_bytes=mib * 1024 * 1024),
     )
 
 
@@ -51,6 +50,43 @@
         return carry
 
     lax.fori_loop(0, live_ref[0], add_tile, 0)
+
+
+def apply_multiply_kernel(
+    live_ref, rows_ref, cols_ref, pairs_ref, used_ref, inverse_ref, image_ref, ppmi_ref, out_ref,
+    top_ref, low_ref, wide_ref, basis_ref,
+):
+    half = inverse_ref.shape[0] // 2
+
+    def split(x):
+        high = x.astype(jnp.bfloat16)
+        return high, (x - high.astype(jnp.float32)).astype(jnp.bfloat16)
+
+    for target, rows, depth in ((top_ref, 0, half), (low_ref, half, 2 * half)):
+        high, rest = split(inverse_ref[pl.ds(rows, half), pl.ds(0, depth)])
+        for k in range(depth // half):
+            part = slice(k * half, (k + 1) * half)
+            for n, piece in enumerate((high, high, rest)):
+                target[:, pl.ds((3 * k + n) * half, half)] = piece[:, part]
+
+    def add_columns(k, carry):
+        first, second = used_ref[2 * k], used_ref[2 * k + 1]
+        for side, c in enumerate((first, second)):
+            lanes = pl.ds(side * TILE, TILE)
+            for part in range(2):
+                high, rest = split(image_ref[c, pl.ds(part * half, half), :])
+                for n, piece in enumerate((high, rest, high)):
+                    wide_ref[pl.ds((3 * part + n) * half, half), lanes] = piece
+        for rows, source, depth in ((0, top_ref, 3 * half), (half, low_ref, 6 * half)):
+            product = jnp.dot(
+                source[...], wide_ref[pl.ds(0, depth), :], preferred_element_type=jnp.float32
+            ).astype(jnp.bfloat16)
+            basis_ref[first, pl.ds(rows, half), :] = product[:, :TILE]
+            basis_ref[second, pl.ds(rows, half), :] = product[:, TILE:]
+        return carry
+
+    lax.fori_loop(0, pairs_ref[0], add_columns, 0)
+    multiply_kernel(live_ref, rows_ref, cols_ref, basis_ref, ppmi_ref, out_ref)
 
 
 def gram_kernel(core_ref, own_ref, other_ref, out_ref):
@@ -124,13 +160,12 @@
                 m[i] = m[i] - cols[k][i - p] * zv[k]
 
 
-def solve_kernel(core_ref, own_ref, other_ref, image_ref, out_ref, a_ref, w_ref):
+def factorize(core_ref, own_ref, other_ref, a_ref, w_ref, step):
     core = core_ref[0]
     for n in range(HALF):
         a_ref[core * HALF + n] = own_ref[n]
         a_ref[(1 - core) * HALF + n] = other_ref[n]
     factor = {}
-    solved = []
     for j in range(BLOCKS):
         here = PLACE[j, j]
 
@@ -148,11 +183,35 @@
             for k in range(j + 1, i + 1):
                 n = PLACE[i, k]
                 a_ref[n] = a_ref[n] - dot_nt(factor[i, j], factor[k, j])
+        step(j, factor, inverse)
+
+
+def solve_kernel(core_ref, own_ref, other_ref, image_ref, out_ref, a_ref, w_ref):
+    solved = []
+
+    def step(j, factor, inverse):
         rest = image_ref[pl.ds(TILE * j, TILE), :]
         for i in range(j):
             rest = rest - dot_nn(factor[j, i], solved[i])
         solved.append(dot_nn(inverse, rest))
         out_ref[pl.ds(TILE * j, TILE), :] = solved[j]
+
+    factorize(core_ref, own_ref, other_ref, a_ref, w_ref, step)
+
+
+def inverse_kernel(core_ref, own_ref, other_ref, out_ref, a_ref, w_ref):
+    out_ref[...] = jnp.zeros_like(out_ref)
+
+    def step(j, factor, inverse):
+        here = pl.ds(TILE * j, TILE)
+        out_ref[here, here] = inverse
+        if j:
+            rest = jnp.zeros((TILE, TILE * j), jnp.float32)
+            for k in range(j):
+                rest = rest - dot_nn(factor[j, k], out_ref[pl.ds(TILE * k, TILE), pl.ds(0, TILE * j)])
+            out_ref[here, pl.ds(0, TILE * j)] = dot_nn(inverse, rest)
+
+    factorize(core_ref, own_ref, other_ref, a_ref, w_ref, step)
 
 
 def swap_core(x):
@@ -204,25 +263,58 @@
     position = jnp.arange(capacity, dtype=jnp.int32)
     keep_mask = (tile_counts > 0) & (position < tile_live[0])[:, None, None]
     ppmi = jnp.where(keep_mask, jnp.maximum(log_ratio, 0.0), 0.0).astype(jnp.bfloat16)
-    multiply = call(
-        multiply_kernel,
-        jax.ShapeDtypeStruct((col_count, width_k, terms_here), jnp.float32),
-        [SMEM, SMEM, SMEM, VMEM, VMEM],
+    column = jnp.arange(row_count, dtype=jnp.int32)
+    live = (position < tile_live[0])[:, None]
+    needed = jnp.any((tile_cols[:, None] == column[None, :]) & live, axis=0)
+    rank = jnp.sum((needed[None, :] & (column[None, :] < column[:, None])).astype(jnp.int32), axis=1)
+    placed = needed[None, :] & (rank[None, :] == column[:, None])
+    used = jnp.sum(jnp.where(placed, column[None, :], 0), axis=1)
+    pairs = ((jnp.sum(needed.astype(jnp.int32)) + 1) // 2).reshape(1)
+    image_parts = jax.ShapeDtypeStruct((col_count, width_k, terms_here), jnp.float32)
+    half = width_k // 2
+    multiply = call(multiply_kernel, image_parts, [SMEM] * 3 + [VMEM] * 2)
+    apply_multiply = call(
+        apply_multiply_kernel,
+        image_parts,
+        [SMEM] * 5 + [VMEM] * 3,
+        [
+            pltpu.VMEM((half, 3 * half), jnp.bfloat16),
+            pltpu.VMEM((half, 6 * half), jnp.bfloat16),
+            pltpu.VMEM((6 * half, 2 * TILE), jnp.bfloat16),
+            pltpu.VMEM((row_count, width_k, terms_here), jnp.bfloat16),
+        ],
+        mib=32,
+    )
+    scratch = [
+        pltpu.VMEM((len(PAIRS), TILE, TILE), jnp.float32),
+        pltpu.VMEM((TILE, TILE), jnp.float32),
+    ]
+    invert = call(
+        inverse_kernel,
+        jax.ShapeDtypeStruct((width_k, width_k), jnp.float32),
+        [SMEM, VMEM, VMEM],
+        scratch,
     )
     solve = call(
         solve_kernel,
         jax.ShapeDtypeStruct((width_k, terms_here), jnp.float32),
         [SMEM, VMEM, VMEM, VMEM],
-        [pltpu.VMEM((len(PAIRS), TILE, TILE), jnp.float32), pltpu.VMEM((TILE, TILE), jnp.float32)],
-    )
+        scratch,
+    )
+    places = (tile_live, tile_rows, tile_cols)
     for sweep_index in range(ITERS):
         if sweep_index:
-            gathered = lax.all_gather(current.astype(jnp.bfloat16), ROWS, axis=0)
-        partial_sum = multiply(tile_live, tile_rows, tile_cols, gathered, ppmi)
+            partial_sum = apply_multiply(*places, pairs, used, inverse, gathered, ppmi)
+        else:
+            partial_sum = multiply(*places, gathered, ppmi)
         image = lax.psum_scatter(partial_sum, "z", scatter_dimension=0)
+        last = sweep_index + 1 == ITERS
+        if not last:
+            gathered = lax.all_gather(image, ROWS, axis=0)
         own, other = gram_sum(core, image)
-        current = solve(core, own, other, image)
-    return current
+        if not last:
+            inverse = invert(core, own, other)
+    return solve(core, own, other, image)
 
 
 def solution(mesh):

time: 371 us -> 324 us (0.87)
  waiting for transfers between devices: 175 us -> 135 us
  blocking collectives: 76.6 us -> 64.6 us
  starting transfers between devices: 19.2 us -> 24.7 us
  local copies, waits for them, and re-layouts: 4.07 us -> 9.46 us
  Pallas kernels: 65.6 us -> 60.4 us
    all_gather x1, waiting for transfers between devices: 44.3 us -> 0.02 us  [local(): gathered = lax.all_gather(image, ROWS, axis=0)]
    all_to_all x2 -> x1, blocking collectives: 23 us -> 11.5 us  [gram_sum(): part = lax.all_to_all(part, PLANE, 0, 0)]
    all_to_all x0 -> x1, waiting for transfers between devices: none -> 8.44 us  [gram_sum(): part = lax.all_to_all(part, PLANE, 0, 0)]
    unnamed x12 -> x14, local copies, waits for them, and re-layouts: 2.84 us -> 7.47 us
    all_to_all x0 -> x1, starting transfers between devices: none -> 3.91 us  [gram_sum(): part = lax.all_to_all(part, PLANE, 0, 0)]
  transfers between devices with their start and end apart: 8 -> 9, of which waited for: 8 -> 7; matrix products, arithmetic and copies ran while one was open for 3% -> 3% of each run, Pallas kernels for 0% -> 7%
where the time goes in v2:
time: 324 us; the launch traced here: 320 us
  waiting for transfers between devices  135 us (42%)
  blocking collectives  64.6 us (20%)
  Pallas kernels  60.4 us (19%)
  starting transfers between devices  24.7 us (8%)
  between operations  15.4 us (5%)
  other arithmetic  10.3 us (3%)
  local copies, waits for them, and re-layouts  9.46 us (3%)
    reduce_scatter x2, waiting for transfers between devices, local(): image = lax.psum_scatter(partial_sum, 'z', scatter_dimension=0)  76 us
    all_gather x1, waiting for transfers between devices, local(): gathered = lax.all_gather(basis.astype(jnp.bfloat16), ROWS, axis=0)  46.9 us
    all_to_all x2, blocking collectives, gram_sum(): part = jnp.sum(lax.all_to_all(part, PLANE, 0, 0), axis=0)  27.9 us
    all_to_all x2, blocking collectives, gram_sum(): part = jnp.sum(lax.all_to_all(part, 'z', 0, 0), axis=0)  25.2 us
    pallas_call x1, Pallas kernels, local(): return solve(core, own, other, image)  22.3 us
    pallas_call x1, Pallas kernels, local(): inverse = invert(core, own, other)  21.1 us
    ppermute x4, starting transfers between devices, swap_core(): return lax.ppermute(x, 'core', [(0, 1), (1, 0)])  20.6 us
    all_to_all x1, blocking collectives, gram_sum(): part = lax.all_to_all(part, PLANE, 0, 0)  11.5 us
  transfers between devices with their start and end apart: 9, of which 7 were waited for; matrix products, arithmetic and copies ran while one was open for 3% of the time, Pallas kernels for 7%

profile of v2, /device:TPU:1, one launch (start us, length us, event | category | flops | bytes accessed | tf_op | source)
XLA Modules:
  0.0 320.1 jit_solution(12289805392467948506)
XLA Ops:
  6.5 0.0 all-gather.6.cloned.1.call-start
  6.5 1.6 convert_element_type.20
  8.2 0.0 copy-start.5
  8.2 0.0 copy-start.6
  8.2 0.0 all-gather.6.cloned.1.call-update
  8.2 0.0 reduce-scatter.3.cloned.1.call-start
  8.9 1.6 convert_reduce_fusion
  11.1 0.7 compare_select_fusion.1
  11.8 0.6 gather_fusion
  12.4 0.7 compare_select_fusion
  13.0 0.6 gather_fusion.1
  13.6 0.7 compare_and_fusion.1
  14.3 0.7 compare_and_fusion
  14.9 0.1 broadcast_select_fusion
  15.0 3.3 %select_convert_fusion.ppmi_ref = bf16[32,128,128]{2,1,0:T(8,128)(2,1)S(1)} fusion(s32[32,128,128]{2,1,0:T(8,128)} %param.7, f32[32,128]{1,0:T(8,128)S(1)} %get-tuple-element.7, f32[32,128]{1,0:T(8,128)S(1)} %get-tuple-element.8, f32[]{:T(128)S(6)} %log.10, pred[32]{0:T(512)(128)(4,1)S(1)} %iota_compare_fusion.3), kind=kLoop, calls=%fused_computation.2 | loop fusion | flops 5242880 | bytes 3178532 | tf_op jit(solution)/shard_map/convert_element_type | solution.py:265
  18.4 46.9 %all-gather.6.cloned.1.call-done = bf16[16384,128]{1,0:T(8,128)(2,1)} async-done(((bf16[512,128]{1,0:T(8,128)(2,1)}), bf16[16384,128]{1,0:T(8,128)(2,1)}) %all-gather.6.cloned.1.call-update) | async-done | bytes 4194320 | tf_op jit(solution)/shard_map/all_gather | solution.py:247
  65.3 0.0 copy-done.5
  65.3 0.0 copy-done.6
  65.3 0.0 copy-start.1
  65.3 2.2 copy-done.1
  67.5 5.1 %shard_map.64 = f32[8,512,128]{2,1,0:T(8,128)} custom-call(s32[1]{0:T(128)} %copy.7.live_ref, s32[32]{0:T(128)S(1)} %copy-done.5, s32[32]{0:T(128)S(1)} %copy-done.6, bf16[32,512,128]{2,1,0:T(8,128)(2,1)S(1)} %bitcast.15, bf16[32,128,128]{2,1,0:T(8,128)(2,1)S(1)} %select_convert_fusion.ppmi_ref), custom_call_target="tpu_custom_call" | custom-call | tf_op jit(solution)/shard_map/pallas_call | solution.py:309
  72.5 0.0 reduce-scatter.3.cloned.1.call-update
  72.6 0.0 all-gather.4.cloned.1.call-start
  72.6 39.2 %reduce-scatter.3.cloned.1.call-done = f32[1,512,128]{2,1,0:T(8,128)} async-done(((f32[8,512,128]{2,1,0:T(8,128)}), f32[1,512,128]{2,1,0:T(8,128)}) %reduce-scatter.3.cloned.1.call-update) | async-done | bytes 262160 | tf_op jit(solution)/shard_map/reduce_scatter | solution.py:310
  111.8 0.0 all-gather.4.cloned.1.call-update
  111.8 5.1 %collective-permute-start = (f32[512,128]{1,0:T(8,128)}, f32[512,128]{1,0:T(8,128)S(1)}, u32[]{:S(2)}, u32[]{:S(2)}) collective-permute-start(f32[512,128]{1,0:T(8,128)} %bitcast.22), channel_id=1, source_target_pairs={{0,8},{8,0},{1,9},{9,1},{2,10},{10,2},{3,11},{11,3},{4,12},{12,4},... | collective-permute-start | bytes 786440 | tf_op jit(solution)/shard_map/ppermute | solution.py:218
  116.9 1.4 collective-permute-done.other_ref
  118.3 0.0 copy-start.2
  118.3 0.9 copy-done.2
  119.2 1.5 shard_map.65
  120.7 13.9 %all_to_all.30 = f32[16,40,128]{2,1,0:T(8,128)S(1)} all-to-all(f32[16,40,128]{2,1,0:T(8,128)S(1)} %bitcast.16), channel_id=1, replica_groups=mesh['x'=4,'y'=4,'core'=2,'z'=8] {'x','y'}, dimensions={0} | all-to-all | bytes 655360 | tf_op jit(solution)/shard_map/all_to_all | solution.py:229
  134.7 12.7 %all_to_all.31 = f32[8,40,128]{2,1,0:T(8,128)S(1)} all-to-all(f32[8,40,128]{2,1,0:T(8,128)S(1)} %broadcast_in_dim.48), channel_id=1, replica_groups=mesh['x'=4,'y'=4,'core'=2,'z'=8] {'z'}, dimensions={0} | all-to-all | bytes 327680 | tf_op jit(solution)/shard_map/all_to_all | solution.py:231
  147.4 0.8 broadcast_in_dim.49
  148.1 3.9 %all-to-all-start.2 = ((f32[16,40,128]{2,1,0:T(8,128)}), f32[16,40,128]{2,1,0:T(8,128)S(1)}, u32[]{:S(2)}, u32[]{:S(2)}) async-start(f32[16,40,128]{2,1,0:T(8,128)} %broadcast_in_dim.49), calls=%async_computation.3 | async-start | bytes 655360 | tf_op jit(solution)/shard_map/all_to_all | solution.py:233
  152.0 0.0 reduce-scatter.5.cloned.1.call-start
  152.1 0.1 fusion.1
  152.2 8.4 %all-to-all-done.2 = f32[16,40,128]{2,1,0:T(8,128)S(1)} async-done(((f32[16,40,128]{2,1,0:T(8,128)}), f32[16,40,128]{2,1,0:T(8,128)S(1)}, u32[]{:S(2)}, u32[]{:S(2)}) %all-to-all-start.2) | async-done | bytes 327712 | tf_op jit(solution)/shard_map/all_to_all | solution.py:233
  160.6 6.0 %collective-permute-start.1 = (f32[5,128,128]{2,1,0:T(8,128)S(1)}, f32[5,128,128]{2,1,0:T(8,128)S(1)}, u32[]{:S(2)}, u32[]{:S(2)}) collective-permute-start(f32[5,128,128]{2,1,0:T(8,128)S(1)} %bitcast.18), channel_id=1, source_target_pairs={{0,8},{8,0},{1,9},{9,1},{2,10},{10,2},{3,11},{11,3},{4,12},{12,4},... | collective-permute-start | bytes 983048 | tf_op jit(solution)/shard_map/ppermute | solution.py:218
  166.6 0.6 convert_reduce_fusion.2
  168.0 0.1 convert_reduce_fusion.1
  168.1 0.1 select_reduce_fusion.used_ref
  168.2 0.0 collective-permute-done.1.other_ref
  168.2 21.1 %shard_map.66.inverse_ref = f32[512,512]{1,0:T(8,128)S(1)} custom-call(s32[1]{0:T(128)} %bitcast.core_ref, f32[5,128,128]{2,1,0:T(8,128)S(1)} %bitcast.19, f32[5,128,128]{2,1,0:T(8,128)S(1)} %collective-permute-done.1.other_ref), custom_call_target="tpu_custom_call" | custom-call | tf_op jit(solution)/shard_map/pallas_call | solution.py:316
  189.3 0.0 all-gather.4.cloned.1.call-done.image_ref
  189.4 0.0 copy-start
  189.4 3.4 %copy-done = f32[32,512,128]{2,1,0:T(8,128)S(1)} copy-done((f32[32,512,128]{2,1,0:T(8,128)S(1)}, f32[32,512,128]{2,1,0:T(8,128)}, u32[]{:S(2)}) %copy-start) | copy-done | bytes 8388632
  192.7 9.0 %shard_map.67 = f32[8,512,128]{2,1,0:T(8,128)} custom-call(s32[1]{0:T(128)} %copy.7.live_ref, s32[32]{0:T(128)S(1)} %copy-done.5, s32[32]{0:T(128)S(1)} %copy-done.6, s32[1]{0:T(128)} %bitcast.2.pairs_ref, s32[32]{0:T(128)S(1)} %select_reduce_fusion.used_ref, f32[512,512]{1,0:T(8,128)S(1)} %shard_map.66.inverse_ref, f32[32,512,128]{2,1,0:T(8,128)S(1)} %copy-done, ...), custom_call_target="tpu_custom_call" | custom-call | tf_op jit(solution)/shard_map/pallas_call | solution.py:307
  201.7 0.0 reduce-scatter.5.cloned.1.call-update
  201.8 36.8 %reduce-scatter.5.cloned.1.call-done = f32[1,512,128]{2,1,0:T(8,128)} async-done(((f32[8,512,128]{2,1,0:T(8,128)}), f32[1,512,128]{2,1,0:T(8,128)}) %reduce-scatter.5.cloned.1.call-update) | async-done | bytes 262160 | tf_op jit(solution)/shard_map/reduce_scatter | solution.py:310
  238.5 5.0 %collective-permute-start.2 = (f32[512,128]{1,0:T(8,128)}, f32[512,128]{1,0:T(8,128)S(1)}, u32[]{:S(2)}, u32[]{:S(2)}) collective-permute-start(f32[512,128]{1,0:T(8,128)} %bitcast.24), channel_id=1, source_target_pairs={{0,8},{8,0},{1,9},{9,1},{2,10},{10,2},{3,11},{11,3},{4,12},{12,4},... | collective-permute-start | bytes 786440 | tf_op jit(solution)/shard_map/ppermute | solution.py:218
  243.5 1.4 collective-permute-done.2.other_ref
  244.9 0.0 copy-start.3
  244.9 0.9 copy-done.3
  245.8 0.0 copy-start.4
  245.9 1.5 shard_map.68
  247.3 14.0 %all_to_all.32 = f32[16,40,128]{2,1,0:T(8,128)S(1)} all-to-all(f32[16,40,128]{2,1,0:T(8,128)S(1)} %bitcast.17), channel_id=1, replica_groups=mesh['x'=4,'y'=4,'core'=2,'z'=8] {'x','y'}, dimensions={0} | all-to-all | bytes 655360 | tf_op jit(solution)/shard_map/all_to_all | solution.py:229
  261.4 12.5 %all_to_all.33 = f32[8,40,128]{2,1,0:T(8,128)S(1)} all-to-all(f32[8,40,128]{2,1,0:T(8,128)S(1)} %broadcast_in_dim.50), channel_id=1, replica_groups=mesh['x'=4,'y'=4,'core'=2,'z'=8] {'z'}, dimensions={0} | all-to-all | bytes 327680 | tf_op jit(solution)/shard_map/all_to_all | solution.py:231
  273.9 11.5 %all_to_all.34 = f32[16,40,128]{2,1,0:T(8,128)S(1)} all-to-all(f32[16,40,128]{2,1,0:T(8,128)S(1)} %broadcast_in_dim.80), channel_id=1, replica_groups=mesh['x'=4,'y'=4,'core'=2,'z'=8] {'x','y'}, dimensions={0} | all-to-all | bytes 655360 | tf_op jit(solution)/shard_map/all_to_all | solution.py:233
  285.4 4.5 %collective-permute-start.3 = (f32[5,128,128]{2,1,0:T(8,128)S(1)}, f32[5,128,128]{2,1,0:T(8,128)S(1)}, u32[]{:S(2)}, u32[]{:S(2)}) collective-permute-start(f32[5,128,128]{2,1,0:T(8,128)S(1)} %bitcast.20), channel_id=1, source_target_pairs={{0,8},{8,0},{1,9},{9,1},{2,10},{10,2},{3,11},{11,3},{4,12},{12,4},... | collective-permute-start | bytes 983048 | tf_op jit(solution)/shard_map/ppermute | solution.py:218
  289.9 1.3 collective-permute-done.3.other_ref
  291.2 0.0 copy-done.4
  291.2 22.3 %shard_map.69 = f32[512,128]{1,0:T(8,128)} custom-call(s32[1]{0:T(128)} %bitcast.core_ref, f32[5,128,128]{2,1,0:T(8,128)S(1)} %bitcast.21, f32[5,128,128]{2,1,0:T(8,128)S(1)} %collective-permute-done.3.other_ref, f32[512,128]{1,0:T(8,128)S(1)} %bitcast.26), custom_call_target="tpu_custom_call" | custom-call | tf_op jit(solution)/shard_map/pallas_call | solution.py:317
  (12 shorter events, 0.2 us)
Async XLA Ops:
  6.5 58.7 %all-gather.6.cloned.1.call-start = ((), (), s32[]{:S(2)}) async-start(), calls=%async_computation.11 | async-start | bytes 4325376 | tf_op jit(solution)/shard_map/all_gather | solution.py:247
  8.2 57.1 %copy-start.5 = (s32[32]{0:T(128)S(1)}, s32[32]{0:T(128)}, u32[]{:S(2)}) copy-start(s32[32]{0:T(128)} %rows_ref.3) | copy-start | bytes 388
  8.2 57.1 %copy-start.6 = (s32[32]{0:T(128)S(1)}, s32[32]{0:T(128)}, u32[]{:S(2)}) copy-start(s32[32]{0:T(128)} %cols_ref.3) | copy-start | bytes 388
  8.2 103.6 %reduce-scatter.3.cloned.1.call-start = ((), (), s32[]{:S(2)}) async-start(), calls=%async_computation.8 | async-start | bytes 2359296 | tf_op jit(solution)/shard_map/reduce_scatter | solution.py:310
  65.3 2.2 copy-start.1
  72.6 116.8 %all-gather.4.cloned.1.call-start = ((), (), s32[]{:S(2)}) async-start(), calls=%async_computation.9 | async-start | bytes 8650752 | tf_op jit(solution)/shard_map/all_gather | solution.py:313
  111.8 6.4 %collective-permute-start = (f32[512,128]{1,0:T(8,128)}, f32[512,128]{1,0:T(8,128)S(1)}, u32[]{:S(2)}, u32[]{:S(2)}) collective-permute-start(f32[512,128]{1,0:T(8,128)} %bitcast.22), channel_id=1, source_target_pairs={{0,8},{8,0},{1,9},{9,1},{2,10},{10,2},{3,11},{11,3},{4,12},{12,4},... | collective-permute-start | bytes 786440 | tf_op jit(solution)/shard_map/ppermute | solution.py:218
  118.3 0.9 copy-start.2
  148.1 12.5 %all-to-all-start.2 = ((f32[16,40,128]{2,1,0:T(8,128)}), f32[16,40,128]{2,1,0:T(8,128)S(1)}, u32[]{:S(2)}, u32[]{:S(2)}) async-start(f32[16,40,128]{2,1,0:T(8,128)} %broadcast_in_dim.49), calls=%async_computation.3 | async-start | bytes 655360 | tf_op jit(solution)/shard_map/all_to_all | solution.py:233
  152.0 86.5 %reduce-scatter.5.cloned.1.call-start = ((), (), s32[]{:S(2)}) async-start(), calls=%async_computation.10 | async-start | bytes 2359296 | tf_op jit(solution)/shard_map/reduce_scatter | solution.py:310
  160.6 7.5 %collective-permute-start.1 = (f32[5,128,128]{2,1,0:T(8,128)S(1)}, f32[5,128,128]{2,1,0:T(8,128)S(1)}, u32[]{:S(2)}, u32[]{:S(2)}) collective-permute-start(f32[5,128,128]{2,1,0:T(8,128)S(1)} %bitcast.18), channel_id=1, source_target_pairs={{0,8},{8,0},{1,9},{9,1},{2,10},{10,2},{3,11},{11,3},{4,12},{12,4},... | collective-permute-start | bytes 983048 | tf_op jit(solution)/shard_map/ppermute | solution.py:218
  189.4 3.4 %copy-start = (f32[32,512,128]{2,1,0:T(8,128)S(1)}, f32[32,512,128]{2,1,0:T(8,128)}, u32[]{:S(2)}) copy-start(f32[32,512,128]{2,1,0:T(8,128)} %all-gather.4.cloned.1.call-done.image_ref) | copy-start | bytes 25165828
  238.5 6.4 %collective-permute-start.2 = (f32[512,128]{1,0:T(8,128)}, f32[512,128]{1,0:T(8,128)S(1)}, u32[]{:S(2)}, u32[]{:S(2)}) collective-permute-start(f32[512,128]{1,0:T(8,128)} %bitcast.24), channel_id=1, source_target_pairs={{0,8},{8,0},{1,9},{9,1},{2,10},{10,2},{3,11},{11,3},{4,12},{12,4},... | collective-permute-start | bytes 786440 | tf_op jit(solution)/shard_map/ppermute | solution.py:218
  244.9 0.9 copy-start.3
  245.8 45.3 %copy-start.4 = (f32[1,512,128]{2,1,0:T(8,128)S(1)}, f32[1,512,128]{2,1,0:T(8,128)}, u32[]{:S(2)}) copy-start(f32[1,512,128]{2,1,0:T(8,128)} %reduce-scatter.5.cloned.1.call-done) | copy-start | bytes 786436
  285.4 5.8 %collective-permute-start.3 = (f32[5,128,128]{2,1,0:T(8,128)S(1)}, f32[5,128,128]{2,1,0:T(8,128)S(1)}, u32[]{:S(2)}, u32[]{:S(2)}) collective-permute-start(f32[5,128,128]{2,1,0:T(8,128)S(1)} %bitcast.20), channel_id=1, source_target_pairs={{0,8},{8,0},{1,9},{9,1},{2,10},{10,2},{3,11},{11,3},{4,12},{12,4},... | collective-permute-start | bytes 983048 | tf_op jit(solution)/shard_map/ppermute | solution.py:218
Sparse Core Ops, SparseCore 0:
  9.9 55.2 all-gather.5
  72.7 39.0 reduce-scatter.2
  114.4 64.3 all-gather.3
  201.9 36.6 reduce-scatter.4
